TPU v7x, 128 devices: a whole 4x4x4 slice. The times are simulated.
128 devices in a mesh: grp: 4 (over z), ep: 32 (over x, y, core).
Axes of the slice: x: 4, y: 4, z: 4, core: 2. Of those that a mesh axis runs over, the one named last changes fastest.
Arguments:
- attention: bfloat16 [16384, 1024], P(('grp', 'ep')), may hold values from -6 to 6
- residual: bfloat16 [16384, 1024], P(('grp', 'ep')), may hold values from -6 to 6
- out_proj: bfloat16 [1024, 1024], P(None, 'grp'), may hold values from -0.1875 to 0.1875
- pre_gain: float32 [1024], replicated, may hold values from 0.25 to 1.75
- post_gain: float32 [1024], replicated, may hold values from 0.25 to 1.75
- slot_gate_up: bfloat16 [32, 1024, 1024], P('ep'), may hold values from -0.1875 to 0.1875
- slot_down: bfloat16 [32, 512, 1024], P('ep'), may hold values from -0.25 to 0.25
- expert_ids: int32 [16384, 8], P(('grp', 'ep')), may hold values from 0 to 31, all different within a row
- copy_choice: int32 [16384, 8], P(('grp', 'ep')), may hold values from 0 to 3
- placement: int32 [32], replicated, may hold values from 0 to 31, each once
- request_age: int32 [16384], P(('grp', 'ep')), may hold values from 0 to 1048575
- decode_flag: int32 [16384], P(('grp', 'ep')), may hold values 0 or 1
- capacity: int32 [4, 32], replicated, may hold values from 4 to 8, as said below
- route_weight: float32 [16384, 8], P(('grp', 'ep')), may hold values from 0.05 to 1
Outputs:
- layer_out: bfloat16 [16384, 1024], P(('grp', 'ep'))
Inputs may be any that keep to these rules, and one draw needn't show every extreme that they name: At least one block has capacity 8. `expert_ids`: each row names 8 different experts. `placement`: each slot holds a different expert.
All inputs are finite; a program needn't handle non-finite values. No bound on the sum of `decode_flag` on one device may be relied on, other than what follows from the above.
Results may differ from a plain program's by a relative error of at most 0.01.
Values may be sent and summed in bfloat16 or wider, within the bound.
A program may use at most 64 MiB of HBM per device.

v0:
```python
import jax
import jax.numpy as jnp
from jax import lax
from jax.sharding import PartitionSpec as P


def rms_scale(values, gain):
    meansq = jnp.mean(values * values, axis=-1, keepdims=True)
    return values * lax.rsqrt(meansq + 1e-06) * gain


def on_device(
    attention,
    residual,
    out_proj,
    pre_gain,
    post_gain,
    slot_gate_up,
    slot_down,
    expert_ids,
    copy_choice,
    placement,
    request_age,
    decode_flag,
    capacity,
    route_weight,
):
    groups = lax.axis_size("grp")
    owners = lax.axis_size("ep")
    devices_all = groups * owners
    rows_here = attention.shape[0]
    features = attention.shape[1]
    picks_row = expert_ids.shape[1]
    cap_size = max(2, rows_here * picks_row // devices_all)
    columns = jnp.dot(
        lax.all_gather(attention, "grp", axis=0, tiled=True),
        out_proj,
        preferred_element_type=jnp.float32,
    )
    attn_proj = lax.all_to_all(columns, "grp", split_axis=0, concat_axis=1, tiled=True)
    hidden_state = (residual.astype(jnp.float32) + attn_proj).astype(jnp.bfloat16)
    normed = rms_scale(hidden_state.astype(jnp.float32), pre_gain).astype(jnp.bfloat16)
    experts_all = placement.shape[0]
    slot_table = jnp.arange(owners, dtype=jnp.int32)
    matches = (placement[None, :] == jnp.arange(experts_all, dtype=jnp.int32)[:, None]).astype(
        jnp.int32
    )
    slot_of = jnp.sum(slot_table[None, :] * matches, axis=1)
    expert_hits = (
        expert_ids[:, :, None] == jnp.arange(experts_all, dtype=jnp.int32)[None, None, :]
    ).astype(jnp.int32)
    target = copy_choice * owners + jnp.sum(expert_hits * slot_of[None, None, :], axis=2)
    priority = decode_flag * 1048576 + request_age
    order = jnp.arange(rows_here, dtype=jnp.int32)
    ahead_mask = (priority[None, :] > priority[:, None]) | (
        priority[None, :] == priority[:, None]
    ) & (order[None, :] < order[:, None])
    target_hits = jnp.sum(
        (target[:, :, None] == jnp.arange(devices_all, dtype=jnp.int32)[None, None, :]).astype(
            jnp.bfloat16
        ),
        axis=1,
    )
    counts = jnp.dot(
        ahead_mask.astype(jnp.bfloat16), target_hits, preferred_element_type=jnp.float32
    )
    position = jnp.take_along_axis(counts, target, axis=1).astype(jnp.int32)
    granted = jnp.take(capacity.reshape(-1), target)
    accepted = position < granted
    total_slots = devices_all * cap_size
    index = jnp.where(accepted, target * cap_size + position, total_slots)
    spread_rows = jnp.broadcast_to(normed[:, None, :], (rows_here, picks_row, features)).reshape(
        rows_here * picks_row, features
    )
    buffer = (
        jnp.zeros((total_slots, features), jnp.bfloat16)
        .at[index.reshape(-1)]
        .set(spread_rows, mode="drop")
    )
    gate_up_local = slot_gate_up[0]
    down_local = slot_down[0]
    hidden_units = down_local.shape[0]
    arrived = lax.all_to_all(
        buffer.reshape(devices_all, cap_size, features),
        ("grp", "ep"),
        split_axis=0,
        concat_axis=0,
        tiled=True,
    )
    flattened = arrived.reshape(-1, features)
    gate_up = jnp.dot(flattened, gate_up_local, preferred_element_type=jnp.float32)
    expert_hidden = (jax.nn.silu(gate_up[:, :hidden_units]) * gate_up[:, hidden_units:]).astype(
        jnp.bfloat16
    )
    produced = jnp.dot(expert_hidden, down_local, preferred_element_type=jnp.float32).astype(
        jnp.bfloat16
    )
    returned = lax.all_to_all(
        produced.reshape(arrived.shape), ("grp", "ep"), split_axis=0, concat_axis=0, tiled=True
    )
    flat_back = returned.reshape(total_slots, features)
    expert_out = flat_back[jnp.minimum(index, total_slots - 1)]
    weights_kept = jnp.where(accepted, route_weight, jnp.float32(0.0))
    mixture = jnp.einsum("rk,rkd->rd", weights_kept, expert_out, preferred_element_type=jnp.float32)
    return rms_scale(hidden_state.astype(jnp.float32) + mixture, post_gain).astype(jnp.bfloat16)


def solution(mesh):
    placed = (
        P(("grp", "ep"), None),
        P(("grp", "ep"), None),
        P(None, "grp"),
        P(),
        P(),
        P("ep", None, None),
        P("ep", None, None),
        P(("grp", "ep"), None),
        P(("grp", "ep"), None),
        P(),
        P(("grp", "ep")),
        P(("grp", "ep")),
        P(),
        P(("grp", "ep"), None),
    )
    return jax.shard_map(
        on_device, mesh=mesh, in_specs=placed, out_specs=P(("grp", "ep"), None), check_vma=False
    )
```

profile of v0, /device:TPU:1, one launch (start us, length us, event | category | flops | bytes accessed | tf_op | source)
XLA Modules:
  0.0 155.6 jit_solution(14246727109927637221)
XLA Ops:
  6.5 0.7 all-gather.2.cloned.1.call-update
  7.3 0.8 select_reduce_fusion.1
  8.0 0.8 select_reduce_fusion
  8.8 0.7 bitcast_or_fusion
  9.8 0.2 fusion.17
  10.1 0.7 multiply_add_fusion.1
  10.7 0.2 fusion.20
  10.9 6.8 %gather_fusion.2 = f32[1024]{0:T(1024)S(1)} fusion(f32[128,128]{1,0:T(8,128)S(1)} %fusion.20, s32[1024]{0:T(1024)S(1)} %reshape.110), kind=kCustom, calls=%fused_computation.2 | custom fusion | bytes 16384 | tf_op jit(solution)/shard_map/jit(take_along_axis)/gather | solution.py:67
  18.2 6.6 %gather_fusion = s32[1024]{0:T(1024)S(1)} fusion(s32[128]{0:T(128)S(1)} %reshape.87, s32[1024]{0:T(1024)S(1)} %broadcast_clamp_fusion.1), kind=kCustom, calls=%fused_computation | custom fusion | bytes 12288 | tf_op jit(solution)/shard_map/jit(_take)/gather | solution.py:68
  24.9 10.7 %all-gather.2.cloned.1.call-done = bf16[512,1024]{1,0:T(8,128)(2,1)} async-done(((bf16[128,1024]{1,0:T(8,128)(2,1)}), bf16[512,1024]{1,0:T(8,128)(2,1)}) %all-gather.2.cloned.1.call-update) | async-done | bytes 1048592 | tf_op jit(solution)/shard_map/all_gather | solution.py:36
  35.6 2.5 %fusion.27 = f32[512,256]{1,0:T(8,128)} fusion(bf16[512,1024]{1,0:T(8,128)(2,1)} %all-gather.2.cloned.1.call-done, bf16[1024,256]{1,0:T(8,128)(2,1)S(1)} %copy-done.1), kind=kOutput, calls=%fused_computation.57 | convolution fusion | flops 268435456 | bytes 2097152 | tf_op jit(solution)/shard_map/dot_general | solution.py:35
  38.1 3.6 %all-to-all-start = ((f32[4,128,256]{2,1,0:T(8,128)}), f32[4,128,256]{2,1,0:T(8,128)S(1)}, u32[]{:S(2)}, u32[]{:S(2)}) async-start(f32[4,128,256]{2,1,0:T(8,128)} %bitcast), calls=%async_computation | async-start | bytes 1048576 | tf_op jit(solution)/shard_map/all_to_all | solution.py:40
  41.9 7.3 %all-to-all-done = f32[4,128,256]{2,1,0:T(8,128)S(1)} async-done(((f32[4,128,256]{2,1,0:T(8,128)}), f32[4,128,256]{2,1,0:T(8,128)S(1)}, u32[]{:S(2)}, u32[]{:S(2)}) %all-to-all-start) | async-done | bytes 524320 | tf_op jit(solution)/shard_map/all_to_all | solution.py:40
  49.2 0.2 fusion.13
  49.6 6.8 %scatter_custom_fusion = bf16[1024,1024]{1,0:T(8,128)(2,1)} fusion(s32[1024]{0:T(1024)S(1)} %bitcast.43, bf16[128,1024]{1,0:T(8,128)(2,1)S(1)} %fusion.15, bf16[]{:T(256)} %constant.29.clone.1), kind=kCustom, calls=%fused_computation.11 | custom fusion | bytes 2359298 | tf_op jit(solution)/shard_map/scatter | solution.py:78
  56.4 40.3 %all_to_all.29 = bf16[128,8,1024]{2,1,0:T(8,128)(2,1)S(1)} all-to-all(bf16[128,8,1024]{2,1,0:T(8,128)(2,1)} %bitcast.40), channel_id=1, replica_groups=mesh['grp'=4,'ep'=32] {'grp','ep'}, dimensions={0} | all-to-all | bytes 4194304 | tf_op jit(solution)/shard_map/all_to_all | solution.py:83
  96.7 2.4 %fusion.3 = f32[1024,1024]{1,0:T(8,128)S(1)} fusion(bf16[1,1024,1024]{2,1,0:T(8,128)(2,1)S(1)} %copy-done, bf16[128,8,1024]{2,1,0:T(8,128)(2,1)S(1)} %all_to_all.29), kind=kOutput, calls=%fused_computation.8 | convolution fusion | flops 2147483648 | bytes 8388608 | tf_op jit(solution)/shard_map/dot_general | solution.py:91
  99.1 2.6 %convert_bitcast_fusion = bf16[128,8,1024]{2,1,0:T(8,128)(2,1)} fusion(f32[1024,1024]{1,0:T(8,128)S(1)} %fusion.3, bf16[1,512,1024]{2,1,0:T(8,128)(2,1)S(1)} %copy-done.7), kind=kOutput, calls=%fused_computation.13 | convolution fusion | flops 1077936128 | bytes 7340032 | tf_op jit(solution)/shard_map/dot_general | solution.py:95
  101.7 5.5 %all-to-all-start.2 = ((bf16[128,8,1024]{2,1,0:T(8,128)(2,1)}), bf16[128,8,1024]{2,1,0:T(8,128)(2,1)}, u32[]{:S(2)}, u32[]{:S(2)}) async-start(bf16[128,8,1024]{2,1,0:T(8,128)(2,1)} %convert_bitcast_fusion), calls=%async_computation.2 | async-start | bytes 4194304 | tf_op jit(solution)/shard_map/all_to_all | solution.py:98
  107.6 29.9 %all-to-all-done.2 = bf16[128,8,1024]{2,1,0:T(8,128)(2,1)} async-done(((bf16[128,8,1024]{2,1,0:T(8,128)(2,1)}), bf16[128,8,1024]{2,1,0:T(8,128)(2,1)}, u32[]{:S(2)}, u32[]{:S(2)}) %all-to-all-start.2) | async-done | bytes 2097184 | tf_op jit(solution)/shard_map/all_to_all | solution.py:98
  137.5 7.9 %gather_fusion.1 = bf16[1024,1024]{1,0:T(8,128)(2,1)} fusion(bf16[1024,1024]{1,0:T(8,128)(2,1)} %bitcast.11, s32[1024]{0:T(1024)S(1)} %broadcast_clamp_fusion), kind=kCustom, calls=%fused_computation.1 | custom fusion | bytes 4198400 | tf_op jit(solution)/shard_map/gather | solution.py:102
  145.5 2.3 %fusion.1 = f32[128,1,1024]{2,1,0:T(1,128)S(1)} fusion(bf16[128,8,1]{1,2,0:T(2,128)(2,1)S(1)} %copy.31, bf16[1024,1024]{1,0:T(8,128)(2,1)} %gather_fusion.1), kind=kOutput, calls=%fused_computation.6 | convolution fusion | flops 2097152 | bytes 2623488 | tf_op jit(solution)/shard_map/rk,rkd->rd/dot_general | solution.py:104
  147.8 0.2 multiply_reduce_fusion
  147.9 0.8 multiply_convert_fusion
  (42 shorter events, 1.6 us)
Async XLA Ops:
  6.5 90.2 %copy-start = (bf16[1,1024,1024]{2,1,0:T(8,128)(2,1)S(1)}, bf16[1,1024,1024]{2,1,0:T(8,128)(2,1)}, u32[]{:S(2)}) copy-start(bf16[1,1024,1024]{2,1,0:T(8,128)(2,1)} %param.19) | copy-start | bytes 6291460
  6.5 29.1 %all-gather.2.cloned.1.call-start = ((), (), s32[]{:S(2)}) async-start(), calls=%async_computation.3 | async-start | bytes 1310720 | tf_op jit(solution)/shard_map/all_gather | solution.py:36
  10.9 7.2 %copy-start.6 = (s32[4,32]{1,0:T(4,128)S(1)}, s32[4,32]{1,0:T(4,128)}, u32[]{:S(2)}) copy-start(s32[4,32]{1,0:T(4,128)} %param.26) | copy-start | bytes 1540
  18.2 17.4 %copy-start.1 = (bf16[1024,256]{1,0:T(8,128)(2,1)S(1)}, bf16[1024,256]{1,0:T(8,128)(2,1)}, u32[]{:S(2)}) copy-start(bf16[1024,256]{1,0:T(8,128)(2,1)} %param.16) | copy-start | bytes 1572868
  24.9 24.3 %copy-start.2 = (bf16[128,1024]{1,0:T(8,128)(2,1)S(1)}, bf16[128,1024]{1,0:T(8,128)(2,1)}, u32[]{:S(2)}) copy-start(bf16[128,1024]{1,0:T(8,128)(2,1)} %param.15) | copy-start | bytes 786436
  38.1 11.3 %copy-start.3 = (f32[1024]{0:T(1024)S(1)}, f32[1024]{0:T(1024)}, u32[]{:S(2)}) copy-start(f32[1024]{0:T(1024)} %param.17) | copy-start | bytes 12292
  38.1 11.1 %all-to-all-start = ((f32[4,128,256]{2,1,0:T(8,128)}), f32[4,128,256]{2,1,0:T(8,128)S(1)}, u32[]{:S(2)}, u32[]{:S(2)}) async-start(f32[4,128,256]{2,1,0:T(8,128)} %bitcast), calls=%async_computation | async-start | bytes 1048576 | tf_op jit(solution)/shard_map/all_to_all | solution.py:40
  96.7 2.4 %copy-start.7 = (bf16[1,512,1024]{2,1,0:T(8,128)(2,1)S(1)}, bf16[1,512,1024]{2,1,0:T(8,128)(2,1)}, u32[]{:S(2)}) copy-start(bf16[1,512,1024]{2,1,0:T(8,128)(2,1)} %param.20) | copy-start | bytes 3145732
  101.7 5.7 %copy-start.5 = (f32[128,8]{0,1:T(8,128)S(1)}, f32[128,8]{0,1:T(8,128)}, u32[]{:S(2)}) copy-start(f32[128,8]{0,1:T(8,128)} %param.27) | copy-start | bytes 12292
  101.7 35.9 %all-to-all-start.2 = ((bf16[128,8,1024]{2,1,0:T(8,128)(2,1)}), bf16[128,8,1024]{2,1,0:T(8,128)(2,1)}, u32[]{:S(2)}, u32[]{:S(2)}) async-start(bf16[128,8,1024]{2,1,0:T(8,128)(2,1)} %convert_bitcast_fusion), calls=%async_computation.2 | async-start | bytes 4194304 | tf_op jit(solution)/shard_map/all_to_all | solution.py:98
  145.5 2.5 %copy-start.4 = (f32[1024]{0:T(1024)S(1)}, f32[1024]{0:T(1024)}, u32[]{:S(2)}) copy-start(f32[1024]{0:T(1024)} %param.18) | copy-start | bytes 12292
Sparse Core Ops, SparseCore 0:
  9.0 26.5 all-gather.1
where the time goes:
time: 156 us
  waiting for transfers between devices  48.6 us (31%)
  blocking collectives  40.3 us (26%)
  local copies, waits for them, and re-layouts  29.5 us (19%)
  between operations  13.6 us (9%)
  matrix products  9.91 us (6%)
  starting transfers between devices  9.14 us (6%)
  other arithmetic  4.53 us (3%)
    all_to_all x1, blocking collectives, on_device(): lax.all_to_all(buffer.reshape(devices_all, cap_size, features), ('grp', '...  40.3 us
    all_to_all x1, waiting for transfers between devices, on_device(): lax.all_to_all(produced.reshape(arrived.shape), ('grp', 'ep'), split_axis...  29.9 us
    all_gather x1, waiting for transfers between devices, on_device(): lax.all_gather(attention, 'grp', axis=0, tiled=True)  10.7 us
    gather x1, local copies, waits for them, and re-layouts, on_device(): expert_out = flat_back[jnp.minimum(index, total_slots - 1)]  7.92 us
    all_to_all x1, waiting for transfers between devices, on_device(): lax.all_to_all(columns, 'grp', split_axis=0, concat_axis=1, tiled=True)  7.26 us
    gather x5, local copies, waits for them, and re-layouts, on_device(): position = jnp.take_along_axis(counts, target, axis=1).astype(jnp.int32)  7.12 us
    scatter x1, local copies, waits for them, and re-layouts, on_device(): buffer = jnp.zeros((total_slots, features), jnp.bfloat16).at[index.reshap...  6.83 us
    gather x3, local copies, waits for them, and re-layouts, on_device(): granted = jnp.take(capacity.reshape(-1), target)  6.7 us
  transfers between devices with their start and end apart: 3, of which 3 were waited for; matrix products, arithmetic and copies ran while one was open for 12% of the time, Pallas kernels for 0%

commit v1 on v0

--- a/solution.py
+++ b/solution.py
@@ -1,7 +1,18 @@
+import functools
 import jax
 import jax.numpy as jnp
 from jax import lax
 from jax.sharding import PartitionSpec as P
+
+
+def turns_enter(vector, group_axis):
+    all_values = jnp.concatenate(
+        lax.all_to_all(jnp.stack(lax.axis_size(group_axis) * [vector]), group_axis, 0, 0), axis=0
+    )
+    return all_values
+
+
+_manage_axis_part = functools.partial(turns_enter, group_axis="grp")
 
 
 def rms_scale(values, gain):
@@ -32,11 +43,7 @@
     features = attention.shape[1]
     picks_row = expert_ids.shape[1]
     cap_size = max(2, rows_here * picks_row // devices_all)
-    columns = jnp.dot(
-        lax.all_gather(attention, "grp", axis=0, tiled=True),
-        out_proj,
-        preferred_element_type=jnp.float32,
-    )
+    columns = jnp.dot(_manage_axis_part(attention), out_proj, preferred_element_type=jnp.float32)
     attn_proj = lax.all_to_all(columns, "grp", split_axis=0, concat_axis=1, tiled=True)
     hidden_state = (residual.astype(jnp.float32) + attn_proj).astype(jnp.bfloat16)
     normed = rms_scale(hidden_state.astype(jnp.float32), pre_gain).astype(jnp.bfloat16)

time: 156 us -> 139 us (0.89)
  between operations: 13.6 us -> 0.27 us
  waiting for transfers between devices: 48.6 us -> 36.3 us
  starting transfers between devices: 9.14 us -> 15.8 us
  local copies, waits for them, and re-layouts: 29.5 us -> 34.2 us
  matrix products: 9.91 us -> 7.47 us
    all_gather x1 -> x0, waiting for transfers between devices: 10.7 us -> none  [on_device(): lax.all_gather(attention, 'grp', axis=0, tiled=True)]
    all_to_all x0 -> x1, starting transfers between devices: none -> 5.86 us  [turns_enter(): lax.all_to_all(jnp.stack(lax.axis_size(group_axis) * [vector]), group_axi...]
    unnamed x0 -> x1, other arithmetic: none -> 2.92 us
    dot_general x2 -> x1, matrix products: 4.76 us -> 2.29 us  [on_device(): jnp.dot(_manage_axis_part(attention), out_proj, preferred_element_type=jn...]
    another operation x0 -> x1, local copies, waits for them, and re-layouts: none -> 2.21 us  [turns_enter(): jnp.stack(lax.axis_size(group_axis) * [vector])]
  transfers between devices with their start and end apart: 3 -> 3, of which waited for: 3 -> 2; matrix products, arithmetic and copies ran while one was open for 12% -> 12% of each run, Pallas kernels for 0% -> 0%
where the time goes in v1:
time: 139 us
  blocking collectives  40.4 us (29%)
  waiting for transfers between devices  36.3 us (26%)
  local copies, waits for them, and re-layouts  34.2 us (25%)
  starting transfers between devices  15.8 us (11%)
  matrix products  7.47 us (5%)
  other arithmetic  4.16 us (3%)
    all_to_all x1, blocking collectives, on_device(): lax.all_to_all(buffer.reshape(devices_all, cap_size, features), ('grp', '...  40.4 us
    all_to_all x1, waiting for transfers between devices, on_device(): lax.all_to_all(produced.reshape(arrived.shape), ('grp', 'ep'), split_axis...  30 us
    gather x1, local copies, waits for them, and re-layouts, on_device(): expert_out = flat_back[jnp.minimum(index, total_slots - 1)]  7.94 us
    gather x5, local copies, waits for them, and re-layouts, on_device(): position = jnp.take_along_axis(counts, target, axis=1).astype(jnp.int32)  7.12 us
    scatter x1, local copies, waits for them, and re-layouts, on_device(): buffer = jnp.zeros((total_slots, features), jnp.bfloat16).at[index.reshap...  6.83 us
    gather x3, local copies, waits for them, and re-layouts, on_device(): granted = jnp.take(capacity.reshape(-1), target)  6.69 us
    all_to_all x1, waiting for transfers between devices, on_device(): lax.all_to_all(columns, 'grp', split_axis=0, concat_axis=1, tiled=True)  6.34 us
    all_to_all x1, starting transfers between devices, turns_enter(): lax.all_to_all(jnp.stack(lax.axis_size(group_axis) * [vector]), group_axi...  5.86 us
  transfers between devices with their start and end apart: 3, of which 2 were waited for; matrix products, arithmetic and copies ran while one was open for 12% of the time, Pallas kernels for 0%

profile of v1, /device:TPU:1, one launch (start us, length us, event | category | flops | bytes accessed | tf_op | source)
XLA Modules:
  0.0 138.6 jit_solution(17095878688669678342)
XLA Ops:
  0.0 2.2 %stack.2 = bf16[4,128,1024]{2,1,0:T(8,128)(2,1)} broadcast(bf16[128,1024]{1,0:T(8,128)(2,1)} %param.14), dimensions={1,2} | broadcast | bytes 1310720 | tf_op jit(solution)/shard_map/stack | solution.py:10
  2.2 5.9 %all-to-all-start = ((bf16[4,128,1024]{2,1,0:T(8,128)(2,1)}), bf16[4,128,1024]{2,1,0:T(8,128)(2,1)S(1)}, u32[]{:S(2)}, u32[]{:S(2)}) async-start(bf16[4,128,1024]{2,1,0:T(8,128)(2,1)} %stack.2), calls=%async_computation | async-start | bytes 2097152 | tf_op jit(solution)/shard_map/all_to_all | solution.py:10
  8.7 0.2 fusion.18
  8.9 0.2 fusion.21
  9.1 6.8 %gather_fusion.2 = f32[1024]{0:T(1024)S(1)} fusion(f32[128,128]{1,0:T(8,128)S(1)} %fusion.21, s32[1024]{0:T(1024)S(1)} %reshape.115), kind=kCustom, calls=%fused_computation.2 | custom fusion | bytes 16384 | tf_op jit(solution)/shard_map/jit(take_along_axis)/gather | solution.py:74
  16.4 6.6 %gather_fusion = s32[1024]{0:T(1024)S(1)} fusion(s32[128]{0:T(128)S(1)} %reshape.92, s32[1024]{0:T(1024)S(1)} %broadcast_clamp_fusion.1), kind=kCustom, calls=%fused_computation | custom fusion | bytes 12288 | tf_op jit(solution)/shard_map/jit(_take)/gather | solution.py:75
  23.1 2.3 %fusion.15 = f32[4,128,256]{2,1,0:T(8,128)} fusion(bf16[4,128,1024]{2,1,0:T(8,128)(2,1)S(1)} %all-to-all-done, bf16[1024,256]{1,0:T(8,128)(2,1)} %param.16), kind=kOutput, calls=%fused_computation.25 | convolution fusion | flops 268435456 | bytes 2097152 | tf_op jit(solution)/shard_map/dot_general | solution.py:46
  25.4 4.4 %all-to-all-start.1 = ((f32[4,128,256]{2,1,0:T(8,128)}), f32[4,128,256]{2,1,0:T(8,128)S(1)}, u32[]{:S(2)}, u32[]{:S(2)}) async-start(f32[4,128,256]{2,1,0:T(8,128)} %fusion.15), calls=%async_computation.1 | async-start | bytes 1048576 | tf_op jit(solution)/shard_map/all_to_all | solution.py:47
  30.0 1.1 copy.25
  31.1 6.3 %all-to-all-done.1 = f32[4,128,256]{2,1,0:T(8,128)S(1)} async-done(((f32[4,128,256]{2,1,0:T(8,128)}), f32[4,128,256]{2,1,0:T(8,128)S(1)}, u32[]{:S(2)}, u32[]{:S(2)}) %all-to-all-start.1) | async-done | bytes 524320 | tf_op jit(solution)/shard_map/all_to_all | solution.py:47
  37.5 0.2 copy.26
  37.7 0.2 fusion.11
  37.8 0.2 fusion.13
  38.2 6.8 %scatter_custom_fusion = bf16[1024,1024]{1,0:T(8,128)(2,1)} fusion(s32[1024]{0:T(1024)S(1)} %bitcast.36, bf16[128,1024]{1,0:T(8,128)(2,1)S(1)} %copy.33, bf16[]{:T(256)} %constant.29.clone.1), kind=kCustom, calls=%fused_computation.10 | custom fusion | bytes 2359298 | tf_op jit(solution)/shard_map/scatter | solution.py:85
  45.0 40.4 %all_to_all.31 = bf16[128,8,1024]{2,1,0:T(8,128)(2,1)S(1)} all-to-all(bf16[128,8,1024]{2,1,0:T(8,128)(2,1)} %bitcast.34), channel_id=1, replica_groups=mesh['grp'=4,'ep'=32] {'grp','ep'}, dimensions={0} | all-to-all | bytes 4194304 | tf_op jit(solution)/shard_map/all_to_all | solution.py:90
  85.4 2.4 %fusion.1 = f32[1024,1024]{1,0:T(8,128)S(1)} fusion(bf16[1,1024,1024]{2,1,0:T(8,128)(2,1)S(1)} %copy-done, bf16[128,8,1024]{2,1,0:T(8,128)(2,1)S(1)} %all_to_all.31), kind=kOutput, calls=%fused_computation.7 | convolution fusion | flops 2147483648 | bytes 8388608 | tf_op jit(solution)/shard_map/dot_general | solution.py:98
  87.8 2.6 %convert_bitcast_fusion = bf16[128,8,1024]{2,1,0:T(8,128)(2,1)} fusion(f32[1024,1024]{1,0:T(8,128)S(1)} %fusion.1, bf16[1,512,1024]{2,1,0:T(8,128)(2,1)S(1)} %copy-done.7), kind=kOutput, calls=%fused_computation.12 | convolution fusion | flops 1077936128 | bytes 7340032 | tf_op jit(solution)/shard_map/dot_general | solution.py:102
  90.4 5.5 %all-to-all-start.3 = ((bf16[128,8,1024]{2,1,0:T(8,128)(2,1)}), bf16[128,8,1024]{2,1,0:T(8,128)(2,1)}, u32[]{:S(2)}, u32[]{:S(2)}) async-start(bf16[128,8,1024]{2,1,0:T(8,128)(2,1)} %convert_bitcast_fusion), calls=%async_computation.3 | async-start | bytes 4194304 | tf_op jit(solution)/shard_map/all_to_all | solution.py:105
  96.3 30.0 %all-to-all-done.3 = bf16[128,8,1024]{2,1,0:T(8,128)(2,1)} async-done(((bf16[128,8,1024]{2,1,0:T(8,128)(2,1)}), bf16[128,8,1024]{2,1,0:T(8,128)(2,1)}, u32[]{:S(2)}, u32[]{:S(2)}) %all-to-all-start.3) | async-done | bytes 2097184 | tf_op jit(solution)/shard_map/all_to_all | solution.py:105
  126.3 7.9 %gather_fusion.1 = bf16[1024,1024]{1,0:T(8,128)(2,1)} fusion(bf16[1024,1024]{1,0:T(8,128)(2,1)} %bitcast.11, s32[1024]{0:T(1024)S(1)} %broadcast_clamp_fusion), kind=kCustom, calls=%fused_computation.1 | custom fusion | bytes 4198400 | tf_op jit(solution)/shard_map/gather | solution.py:109
  134.2 2.9 %multiply_reduce_fusion = f32[128,1024]{1,0:T(8,128)S(1)} fusion(f32[128,8]{1,0:T(8,128)S(1)} %copy.40, bf16[1024,1024]{1,0:T(8,128)(2,1)} %gather_fusion.1), kind=kLoop, calls=%fused_computation.4 | loop fusion | flops 3014656 | bytes 2625536
  137.1 0.2 copy.39
  137.5 0.2 multiply_convert_fusion
  137.7 0.9 copy.35
  (52 shorter events, 2.0 us)
Async XLA Ops:
  0.0 85.4 %copy-start = (bf16[1,1024,1024]{2,1,0:T(8,128)(2,1)S(1)}, bf16[1,1024,1024]{2,1,0:T(8,128)(2,1)}, u32[]{:S(2)}) copy-start(bf16[1,1024,1024]{2,1,0:T(8,128)(2,1)} %param.19) | copy-start | bytes 6291460
  0.0 8.1 %copy-start.8 = (s32[32]{0:T(128)S(1)}, s32[32]{0:T(128)}, u32[]{:S(2)}) copy-start(s32[32]{0:T(128)} %param.23) | copy-start | bytes 388
  0.0 8.2 %copy-start.3 = (s32[128,8]{0,1:T(8,128)S(1)}, s32[128,8]{0,1:T(8,128)}, u32[]{:S(2)}) copy-start(s32[128,8]{0,1:T(8,128)} %param.21) | copy-start | bytes 12292
  0.0 8.3 %copy-start.5 = (s32[128,8]{0,1:T(8,128)S(1)}, s32[128,8]{0,1:T(8,128)}, u32[]{:S(2)}) copy-start(s32[128,8]{0,1:T(8,128)} %param.22) | copy-start | bytes 12292
  0.0 8.6 %copy-start.9 = (s32[128]{0:T(128)S(1)}, s32[128]{0:T(128)}, u32[]{:S(2)}) copy-start(s32[128]{0:T(128)} %param.24) | copy-start | bytes 1540
  0.0 8.6 %copy-start.10 = (s32[128]{0:T(128)S(1)}, s32[128]{0:T(128)}, u32[]{:S(2)}) copy-start(s32[128]{0:T(128)} %param.25) | copy-start | bytes 1540
  2.2 20.9 %all-to-all-start = ((bf16[4,128,1024]{2,1,0:T(8,128)(2,1)}), bf16[4,128,1024]{2,1,0:T(8,128)(2,1)S(1)}, u32[]{:S(2)}, u32[]{:S(2)}) async-start(bf16[4,128,1024]{2,1,0:T(8,128)(2,1)} %stack.2), calls=%async_computation | async-start | bytes 2097152 | tf_op jit(solution)/shard_map/all_to_all | solution.py:10
  9.1 7.2 %copy-start.6 = (s32[4,32]{1,0:T(4,128)S(1)}, s32[4,32]{1,0:T(4,128)}, u32[]{:S(2)}) copy-start(s32[4,32]{1,0:T(4,128)} %param.26) | copy-start | bytes 1540
  25.4 12.4 %copy-start.1 = (f32[1024]{0:T(1024)S(1)}, f32[1024]{0:T(1024)}, u32[]{:S(2)}) copy-start(f32[1024]{0:T(1024)} %param.17) | copy-start | bytes 12292
  25.4 12.1 %all-to-all-start.1 = ((f32[4,128,256]{2,1,0:T(8,128)}), f32[4,128,256]{2,1,0:T(8,128)S(1)}, u32[]{:S(2)}, u32[]{:S(2)}) async-start(f32[4,128,256]{2,1,0:T(8,128)} %fusion.15), calls=%async_computation.1 | async-start | bytes 1048576 | tf_op jit(solution)/shard_map/all_to_all | solution.py:47
  85.4 2.4 %copy-start.7 = (bf16[1,512,1024]{2,1,0:T(8,128)(2,1)S(1)}, bf16[1,512,1024]{2,1,0:T(8,128)(2,1)}, u32[]{:S(2)}) copy-start(bf16[1,512,1024]{2,1,0:T(8,128)(2,1)} %param.20) | copy-start | bytes 3145732
  90.4 5.8 %copy-start.4 = (f32[128,8]{0,1:T(8,128)S(1)}, f32[128,8]{0,1:T(8,128)}, u32[]{:S(2)}) copy-start(f32[128,8]{0,1:T(8,128)} %param.27) | copy-start | bytes 12292
  90.4 35.8 %all-to-all-start.3 = ((bf16[128,8,1024]{2,1,0:T(8,128)(2,1)}), bf16[128,8,1024]{2,1,0:T(8,128)(2,1)}, u32[]{:S(2)}, u32[]{:S(2)}) async-start(bf16[128,8,1024]{2,1,0:T(8,128)(2,1)} %convert_bitcast_fusion), calls=%async_computation.3 | async-start | bytes 4194304 | tf_op jit(solution)/shard_map/all_to_all | solution.py:105
  134.2 3.3 %copy-start.2 = (f32[1024]{0:T(1024)S(1)}, f32[1024]{0:T(1024)}, u32[]{:S(2)}) copy-start(f32[1024]{0:T(1024)} %param.18) | copy-start | bytes 12292
